TPU v7x, 32 devices: a whole 2x2x4 slice. The times are simulated.
32 devices in a mesh: slab: 2 (over x), tile: 8 (over z, y), ch: 2 (over core).
Axes of the slice: x: 2, y: 2, z: 4, core: 2. Of those that a mesh axis runs over, the one named last changes fastest.
Arguments:
- volume: bfloat16 [4, 128, 1024], P('slab', 'tile'), may hold values from -6 to 6
- xz_tissue: int32 [128], P('tile'), may hold values 0 or 1
- yz_tissue: int32 [1024], P(('slab', 'tile')), may hold values 0 or 1
- first_conv: bfloat16 [32, 9, 1], replicated, may hold values from -2 to 2
- second_conv: bfloat16 [32, 9, 32], replicated, may hold values from -0.375 to 0.375
- third_conv: bfloat16 [64, 9, 32], replicated, may hold values from -0.375 to 0.375
- fourth_conv: bfloat16 [64, 9, 64], replicated, may hold values from -0.25 to 0.25
- fifth_conv: bfloat16 [32, 9, 96], replicated, may hold values from -0.21875 to 0.21875
- sixth_conv: bfloat16 [32, 9, 32], replicated, may hold values from -0.375 to 0.375
- out_weight: bfloat16 [32], replicated, may hold values from -1 to 1
Outputs:
- restored: bfloat16 [4, 128, 1024], P('slab', 'tile')
All inputs are finite; a program needn't handle non-finite values. No bound on the sum of `xz_tissue` or of `yz_tissue` on one device may be relied on, other than what follows from the above.
Results may differ from a plain program's by a relative error of at most 0.0037.
Values may be sent and summed in bfloat16 or wider, within the bound.
A program may use at most 128 MiB of HBM per device.

v0:
```python
import jax
import jax.numpy as jnp
from jax import lax
from jax.sharding import PartitionSpec as P


def convolve(signal, matrix):
    channels, height, breadth = signal.shape
    padded = jnp.pad(signal, ((0, 0), (1, 1), (1, 1)))
    stacked = jnp.stack(
        [
            padded[:, row_shift : row_shift + height, col_shift : col_shift + breadth]
            for row_shift in range(3)
            for col_shift in range(3)
        ],
        axis=0,
    )
    stacked = stacked.reshape(9 * channels, height, breadth)
    return jnp.einsum("ok,khw->ohw", matrix, stacked, preferred_element_type=jnp.float32)


def whole_layer(signal, weight):
    matrix = weight.reshape(weight.shape[0], -1)
    return jax.nn.relu(convolve(signal, matrix)).astype(jnp.bfloat16)


def shrink(signal):
    channels, height, breadth = signal.shape
    blocks = signal.astype(jnp.float32).reshape(channels, height // 2, 2, breadth // 2, 2)
    return jnp.mean(blocks, axis=(2, 4)).astype(jnp.bfloat16)


def enlarge(signal):
    return jnp.repeat(jnp.repeat(signal, 2, axis=1), 2, axis=2)


def network(picture, weights, layer):
    first_conv, second_conv, third_conv, fourth_conv, fifth_conv, sixth_conv, out_weight = weights
    opening = layer(picture[None], first_conv)
    skipped = layer(opening, second_conv)
    coarse = layer(shrink(skipped), third_conv)
    coarse = layer(coarse, fourth_conv)
    joined = jnp.concatenate([enlarge(coarse), skipped], axis=0)
    refined = layer(joined, fifth_conv)
    refined = layer(refined, sixth_conv)
    head = jnp.einsum("c,chw->hw", out_weight, refined, preferred_element_type=jnp.float32)
    return picture.astype(jnp.float32) + head


def restore(planes, tissue, weights):
    own_count = planes.shape[0] // lax.axis_size("ch")
    own_start = lax.axis_index("ch") * own_count
    own_planes = lax.dynamic_slice_in_dim(planes, own_start, own_count, 0)
    own_tissue = lax.dynamic_slice_in_dim(tissue, own_start, own_count, 0)

    def single(entry):
        picture, marker = entry
        return lax.cond(
            marker > 0,
            lambda source: network(source, weights, whole_layer).astype(jnp.bfloat16),
            lambda source: source,
            picture,
        )

    finished = lax.map(single, (own_planes, own_tissue))
    return lax.all_gather(finished, "ch", axis=0, tiled=True)


def per_device(
    volume,
    xz_tissue,
    yz_tissue,
    first_conv,
    second_conv,
    third_conv,
    fourth_conv,
    fifth_conv,
    sixth_conv,
    out_weight,
):
    weights = (first_conv, second_conv, third_conv, fourth_conv, fifth_conv, sixth_conv, out_weight)
    slabs = lax.axis_size("slab")
    tiles = lax.axis_size("tile")
    depth_dev, rows_dev, across = volume.shape
    xz_turned = lax.all_to_all(volume, "slab", split_axis=1, concat_axis=0, tiled=True)
    xz_planes = jnp.transpose(xz_turned, (1, 0, 2))
    per_slab = rows_dev // slabs
    xz_marks = lax.dynamic_slice_in_dim(xz_tissue, lax.axis_index("slab") * per_slab, per_slab, 0)
    xz_done = restore(xz_planes, xz_marks, weights)
    xz_result = lax.all_to_all(
        jnp.transpose(xz_done, (1, 0, 2)), "slab", split_axis=0, concat_axis=1, tiled=True
    )
    pieces = across // (slabs * tiles)
    grid_shape = (depth_dev, rows_dev, slabs, tiles, pieces)
    grid = volume.reshape(grid_shape)
    moved = lax.all_to_all(
        lax.all_to_all(grid, "slab", split_axis=2, concat_axis=2, tiled=True),
        "tile",
        split_axis=3,
        concat_axis=3,
        tiled=True,
    )
    yz_planes = jnp.transpose(moved, (4, 2, 0, 3, 1)).reshape(
        pieces, slabs * depth_dev, tiles * rows_dev
    )
    yz_done = restore(yz_planes, yz_tissue, weights)
    yz_grid = jnp.transpose(
        yz_done.reshape(pieces, slabs, depth_dev, tiles, rows_dev), (2, 4, 1, 3, 0)
    )
    yz_back = lax.all_to_all(
        lax.all_to_all(yz_grid, "slab", split_axis=2, concat_axis=2, tiled=True),
        "tile",
        split_axis=3,
        concat_axis=3,
        tiled=True,
    )
    yz_result = yz_back.reshape(depth_dev, rows_dev, across)
    averaged = 0.5 * (xz_result.astype(jnp.float32) + yz_result.astype(jnp.float32))
    return averaged.astype(jnp.bfloat16)


def solution(mesh):
    return jax.shard_map(
        per_device,
        mesh=mesh,
        in_specs=(
            P("slab", "tile", None),
            P("tile"),
            P(("slab", "tile")),
            P(),
            P(),
            P(),
            P(),
            P(),
            P(),
            P(),
        ),
        out_specs=P("slab", "tile", None),
        check_vma=False,
    )
```

profile of v0, /device:TPU:24, one launch (start us, length us, event | category | flops | bytes accessed | tf_op | source)
XLA Modules:
  0.0 260.9 jit_solution(3633319303962851445)
XLA Ops:
  16.8 6.1 %all-to-all-start.3 = ((bf16[8,2,2048]{2,1,0:T(2,128)(2,1)}), bf16[8,2,2048]{2,1,0:T(2,128)(2,1)S(1)}, u32[]{:S(2)}, u32[]{:S(2)}) async-start(bf16[8,2,2048]{2,1,0:T(2,128)(2,1)} %reshape.148), calls=%async_computation.3 | async-start | bytes 131072 | tf_op jit(solution)/shard_map/all_to_all | solution.py:96
  27.0 129.9 %while.21 = (s32[]{:T(128)}, bf16[32,4,128]{2,1,0:T(4,128)(2,1)S(1)}, s32[32]{0:T(128)S(1)}, bf16[32,4,128]{2,1,0:T(4,128)(2,1)S(1)}, bf16[32,9,1]{0,1,2:T(8,128...) while((s32[]{:T(128)}, ...), condition=%wide.region_9.10_spmd, body=%wide.region_5.9_spmd.sunk | while | flops 62256644 | bytes 6667115 | solution.py:65
  28.2 5.5 %conditional.5 = (bf16[1,4,128]{2,1,0:T(4,128)(2,1)S(1)}) conditional(s32[]{:T(128)} %bitcast.693, bf16[4,128]{1,0:T(4,128)(2,1)S(1)} %dynamic-slice_bitcast_fusion.6, (bf16[4,128]{1,0:T(4,128)(2,1)S(1)}, bf16[32,9,1]{0,1,2:T(8,128)(2,1)S(1)}, bf16[32,9,32]{2,0,1:T(8,128)(2,1)S(1)}, bf16[64,9,32]{0,2,1:T(8,128)(2,1)S(1)}, ...), branch_computations={%region_6.6_spmd, %region_7.8_spmd} | conditional | flops 62256640 | bytes 6662796 | solution.py:58
  37.7 5.5 %conditional.5 = (bf16[1,4,128]{2,1,0:T(4,128)(2,1)S(1)}) conditional(s32[]{:T(128)} %bitcast.693, bf16[4,128]{1,0:T(4,128)(2,1)S(1)} %dynamic-slice_bitcast_fusion.6, (bf16[4,128]{1,0:T(4,128)(2,1)S(1)}, bf16[32,9,1]{0,1,2:T(8,128)(2,1)S(1)}, bf16[32,9,32]{2,0,1:T(8,128)(2,1)S(1)}, bf16[64,9,32]{0,2,1:T(8,128)(2,1)S(1)}, ...), branch_computations={%region_6.6_spmd, %region_7.8_spmd} | conditional | flops 62256640 | bytes 6662796 | solution.py:58
  45.8 5.5 %conditional.5 = (bf16[1,4,128]{2,1,0:T(4,128)(2,1)S(1)}) conditional(s32[]{:T(128)} %bitcast.693, bf16[4,128]{1,0:T(4,128)(2,1)S(1)} %dynamic-slice_bitcast_fusion.6, (bf16[4,128]{1,0:T(4,128)(2,1)S(1)}, bf16[32,9,1]{0,1,2:T(8,128)(2,1)S(1)}, bf16[32,9,32]{2,0,1:T(8,128)(2,1)S(1)}, bf16[64,9,32]{0,2,1:T(8,128)(2,1)S(1)}, ...), branch_computations={%region_6.6_spmd, %region_7.8_spmd} | conditional | flops 62256640 | bytes 6662796 | solution.py:58
  53.9 5.5 %conditional.5 = (bf16[1,4,128]{2,1,0:T(4,128)(2,1)S(1)}) conditional(s32[]{:T(128)} %bitcast.693, bf16[4,128]{1,0:T(4,128)(2,1)S(1)} %dynamic-slice_bitcast_fusion.6, (bf16[4,128]{1,0:T(4,128)(2,1)S(1)}, bf16[32,9,1]{0,1,2:T(8,128)(2,1)S(1)}, bf16[32,9,32]{2,0,1:T(8,128)(2,1)S(1)}, bf16[64,9,32]{0,2,1:T(8,128)(2,1)S(1)}, ...), branch_computations={%region_6.6_spmd, %region_7.8_spmd} | conditional | flops 62256640 | bytes 6662796 | solution.py:58
  60.7 5.5 %conditional.5 = (bf16[1,4,128]{2,1,0:T(4,128)(2,1)S(1)}) conditional(s32[]{:T(128)} %bitcast.693, bf16[4,128]{1,0:T(4,128)(2,1)S(1)} %dynamic-slice_bitcast_fusion.6, (bf16[4,128]{1,0:T(4,128)(2,1)S(1)}, bf16[32,9,1]{0,1,2:T(8,128)(2,1)S(1)}, bf16[32,9,32]{2,0,1:T(8,128)(2,1)S(1)}, bf16[64,9,32]{0,2,1:T(8,128)(2,1)S(1)}, ...), branch_computations={%region_6.6_spmd, %region_7.8_spmd} | conditional | flops 62256640 | bytes 6662796 | solution.py:58
  72.7 5.5 %conditional.5 = (bf16[1,4,128]{2,1,0:T(4,128)(2,1)S(1)}) conditional(s32[]{:T(128)} %bitcast.693, bf16[4,128]{1,0:T(4,128)(2,1)S(1)} %dynamic-slice_bitcast_fusion.6, (bf16[4,128]{1,0:T(4,128)(2,1)S(1)}, bf16[32,9,1]{0,1,2:T(8,128)(2,1)S(1)}, bf16[32,9,32]{2,0,1:T(8,128)(2,1)S(1)}, bf16[64,9,32]{0,2,1:T(8,128)(2,1)S(1)}, ...), branch_computations={%region_6.6_spmd, %region_7.8_spmd} | conditional | flops 62256640 | bytes 6662796 | solution.py:58
  79.5 5.5 %conditional.5 = (bf16[1,4,128]{2,1,0:T(4,128)(2,1)S(1)}) conditional(s32[]{:T(128)} %bitcast.693, bf16[4,128]{1,0:T(4,128)(2,1)S(1)} %dynamic-slice_bitcast_fusion.6, (bf16[4,128]{1,0:T(4,128)(2,1)S(1)}, bf16[32,9,1]{0,1,2:T(8,128)(2,1)S(1)}, bf16[32,9,32]{2,0,1:T(8,128)(2,1)S(1)}, bf16[64,9,32]{0,2,1:T(8,128)(2,1)S(1)}, ...), branch_computations={%region_6.6_spmd, %region_7.8_spmd} | conditional | flops 62256640 | bytes 6662796 | solution.py:58
  86.4 5.5 %conditional.5 = (bf16[1,4,128]{2,1,0:T(4,128)(2,1)S(1)}) conditional(s32[]{:T(128)} %bitcast.693, bf16[4,128]{1,0:T(4,128)(2,1)S(1)} %dynamic-slice_bitcast_fusion.6, (bf16[4,128]{1,0:T(4,128)(2,1)S(1)}, bf16[32,9,1]{0,1,2:T(8,128)(2,1)S(1)}, bf16[32,9,32]{2,0,1:T(8,128)(2,1)S(1)}, bf16[64,9,32]{0,2,1:T(8,128)(2,1)S(1)}, ...), branch_computations={%region_6.6_spmd, %region_7.8_spmd} | conditional | flops 62256640 | bytes 6662796 | solution.py:58
  95.8 5.5 %conditional.5 = (bf16[1,4,128]{2,1,0:T(4,128)(2,1)S(1)}) conditional(s32[]{:T(128)} %bitcast.693, bf16[4,128]{1,0:T(4,128)(2,1)S(1)} %dynamic-slice_bitcast_fusion.6, (bf16[4,128]{1,0:T(4,128)(2,1)S(1)}, bf16[32,9,1]{0,1,2:T(8,128)(2,1)S(1)}, bf16[32,9,32]{2,0,1:T(8,128)(2,1)S(1)}, bf16[64,9,32]{0,2,1:T(8,128)(2,1)S(1)}, ...), branch_computations={%region_6.6_spmd, %region_7.8_spmd} | conditional | flops 62256640 | bytes 6662796 | solution.py:58
  102.6 5.5 %conditional.5 = (bf16[1,4,128]{2,1,0:T(4,128)(2,1)S(1)}) conditional(s32[]{:T(128)} %bitcast.693, bf16[4,128]{1,0:T(4,128)(2,1)S(1)} %dynamic-slice_bitcast_fusion.6, (bf16[4,128]{1,0:T(4,128)(2,1)S(1)}, bf16[32,9,1]{0,1,2:T(8,128)(2,1)S(1)}, bf16[32,9,32]{2,0,1:T(8,128)(2,1)S(1)}, bf16[64,9,32]{0,2,1:T(8,128)(2,1)S(1)}, ...), branch_computations={%region_6.6_spmd, %region_7.8_spmd} | conditional | flops 62256640 | bytes 6662796 | solution.py:58
  109.4 5.5 %conditional.5 = (bf16[1,4,128]{2,1,0:T(4,128)(2,1)S(1)}) conditional(s32[]{:T(128)} %bitcast.693, bf16[4,128]{1,0:T(4,128)(2,1)S(1)} %dynamic-slice_bitcast_fusion.6, (bf16[4,128]{1,0:T(4,128)(2,1)S(1)}, bf16[32,9,1]{0,1,2:T(8,128)(2,1)S(1)}, bf16[32,9,32]{2,0,1:T(8,128)(2,1)S(1)}, bf16[64,9,32]{0,2,1:T(8,128)(2,1)S(1)}, ...), branch_computations={%region_6.6_spmd, %region_7.8_spmd} | conditional | flops 62256640 | bytes 6662796 | solution.py:58
  118.8 5.5 %conditional.5 = (bf16[1,4,128]{2,1,0:T(4,128)(2,1)S(1)}) conditional(s32[]{:T(128)} %bitcast.693, bf16[4,128]{1,0:T(4,128)(2,1)S(1)} %dynamic-slice_bitcast_fusion.6, (bf16[4,128]{1,0:T(4,128)(2,1)S(1)}, bf16[32,9,1]{0,1,2:T(8,128)(2,1)S(1)}, bf16[32,9,32]{2,0,1:T(8,128)(2,1)S(1)}, bf16[64,9,32]{0,2,1:T(8,128)(2,1)S(1)}, ...), branch_computations={%region_6.6_spmd, %region_7.8_spmd} | conditional | flops 62256640 | bytes 6662796 | solution.py:58
  125.6 5.5 %conditional.5 = (bf16[1,4,128]{2,1,0:T(4,128)(2,1)S(1)}) conditional(s32[]{:T(128)} %bitcast.693, bf16[4,128]{1,0:T(4,128)(2,1)S(1)} %dynamic-slice_bitcast_fusion.6, (bf16[4,128]{1,0:T(4,128)(2,1)S(1)}, bf16[32,9,1]{0,1,2:T(8,128)(2,1)S(1)}, bf16[32,9,32]{2,0,1:T(8,128)(2,1)S(1)}, bf16[64,9,32]{0,2,1:T(8,128)(2,1)S(1)}, ...), branch_computations={%region_6.6_spmd, %region_7.8_spmd} | conditional | flops 62256640 | bytes 6662796 | solution.py:58
  136.4 5.5 %conditional.5 = (bf16[1,4,128]{2,1,0:T(4,128)(2,1)S(1)}) conditional(s32[]{:T(128)} %bitcast.693, bf16[4,128]{1,0:T(4,128)(2,1)S(1)} %dynamic-slice_bitcast_fusion.6, (bf16[4,128]{1,0:T(4,128)(2,1)S(1)}, bf16[32,9,1]{0,1,2:T(8,128)(2,1)S(1)}, bf16[32,9,32]{2,0,1:T(8,128)(2,1)S(1)}, bf16[64,9,32]{0,2,1:T(8,128)(2,1)S(1)}, ...), branch_computations={%region_6.6_spmd, %region_7.8_spmd} | conditional | flops 62256640 | bytes 6662796 | solution.py:58
  143.2 5.5 %conditional.5 = (bf16[1,4,128]{2,1,0:T(4,128)(2,1)S(1)}) conditional(s32[]{:T(128)} %bitcast.693, bf16[4,128]{1,0:T(4,128)(2,1)S(1)} %dynamic-slice_bitcast_fusion.6, (bf16[4,128]{1,0:T(4,128)(2,1)S(1)}, bf16[32,9,1]{0,1,2:T(8,128)(2,1)S(1)}, bf16[32,9,32]{2,0,1:T(8,128)(2,1)S(1)}, bf16[64,9,32]{0,2,1:T(8,128)(2,1)S(1)}, ...), branch_computations={%region_6.6_spmd, %region_7.8_spmd} | conditional | flops 62256640 | bytes 6662796 | solution.py:58
  151.3 5.5 %conditional.5 = (bf16[1,4,128]{2,1,0:T(4,128)(2,1)S(1)}) conditional(s32[]{:T(128)} %bitcast.693, bf16[4,128]{1,0:T(4,128)(2,1)S(1)} %dynamic-slice_bitcast_fusion.6, (bf16[4,128]{1,0:T(4,128)(2,1)S(1)}, bf16[32,9,1]{0,1,2:T(8,128)(2,1)S(1)}, bf16[32,9,32]{2,0,1:T(8,128)(2,1)S(1)}, bf16[64,9,32]{0,2,1:T(8,128)(2,1)S(1)}, ...), branch_computations={%region_6.6_spmd, %region_7.8_spmd} | conditional | flops 62256640 | bytes 6662796 | solution.py:58
  168.0 28.2 %all-to-all-start.5 = ((bf16[8,2,2048]{2,1,0:T(2,128)(2,1)}), bf16[8,2,2048]{2,1,0:T(2,128)(2,1)S(1)}, u32[]{:S(2)}, u32[]{:S(2)}) async-start(bf16[8,2,2048]{2,1,0:T(2,128)(2,1)} %reshape.152), calls=%async_computation.5 | async-start | bytes 131072 | tf_op jit(solution)/shard_map/all_to_all | solution.py:110
  196.2 43.2 %while.20 = (s32[]{:T(128)}, bf16[4,4,1024]{2,1,0:T(4,128)(2,1)S(1)}, s32[4]{0:T(128)S(1)}, bf16[4,4,1024]{2,1,0:T(4,128)(2,1)S(1)}, bf16[32,9,1]{0,1,2:T(8,128)...) while((s32[]{:T(128)}, ...), condition=%wide.region_4.5_spmd, body=%wide.region_0.4_spmd.sunk | while | flops 498053120 | bytes 48503660 | solution.py:65
  197.5 12.6 %conditional.4 = (bf16[1,4,1024]{2,1,0:T(4,128)(2,1)S(1)}) conditional(s32[]{:T(128)} %bitcast.691, bf16[4,1024]{1,0:T(4,128)(2,1)S(1)} %dynamic-slice_bitcast_fusion.5, (bf16[4,1024]{1,0:T(4,128)(2,1)S(1)}, bf16[32,9,1]{0,1,2:T(8,128)(2,1)S(1)}, bf16[32,9,32]{2,0,1:T(8,128)(2,1)S(1)}, bf16[64,9,32]{0,2,1:T(8,128)(2,1)S(1)}, ...), branch_computations={%region_1.1_spmd, %region_2.3_spmd} | conditional | flops 498053120 | bytes 48470668 | solution.py:58
  211.5 12.6 %conditional.4 = (bf16[1,4,1024]{2,1,0:T(4,128)(2,1)S(1)}) conditional(s32[]{:T(128)} %bitcast.691, bf16[4,1024]{1,0:T(4,128)(2,1)S(1)} %dynamic-slice_bitcast_fusion.5, (bf16[4,1024]{1,0:T(4,128)(2,1)S(1)}, bf16[32,9,1]{0,1,2:T(8,128)(2,1)S(1)}, bf16[32,9,32]{2,0,1:T(8,128)(2,1)S(1)}, bf16[64,9,32]{0,2,1:T(8,128)(2,1)S(1)}, ...), branch_computations={%region_1.1_spmd, %region_2.3_spmd} | conditional | flops 498053120 | bytes 48470668 | solution.py:58
  226.7 12.6 %conditional.4 = (bf16[1,4,1024]{2,1,0:T(4,128)(2,1)S(1)}) conditional(s32[]{:T(128)} %bitcast.691, bf16[4,1024]{1,0:T(4,128)(2,1)S(1)} %dynamic-slice_bitcast_fusion.5, (bf16[4,1024]{1,0:T(4,128)(2,1)S(1)}, bf16[32,9,1]{0,1,2:T(8,128)(2,1)S(1)}, bf16[32,9,32]{2,0,1:T(8,128)(2,1)S(1)}, bf16[64,9,32]{0,2,1:T(8,128)(2,1)S(1)}, ...), branch_computations={%region_1.1_spmd, %region_2.3_spmd} | conditional | flops 498053120 | bytes 48470668 | solution.py:58
  239.4 12.8 %all_gather.6 = bf16[8,4,1024]{2,1,0:T(4,128)(2,1)S(1)} all-gather(bf16[4,4,1024]{2,1,0:T(4,128)(2,1)S(1)} %get-tuple-element.187), channel_id=1, replica_groups=mesh['slab'=2,'tile'=8,'ch'=2] {'ch'}, dimensions={0}, use_global_device_ids=true | all-gather | bytes 98304 | tf_op jit(solution)/shard_map/all_gather | solution.py:66
  (1547 shorter events, 183.6 us)
Async XLA Ops:
  0.0 26.9 %copy-start.5 = (bf16[32,9,1]{0,1,2:T(8,128)(2,1)S(1)}, bf16[32,9,1]{0,1,2:T(8,128)(2,1)}, u32[]{:S(2)}) copy-start(bf16[32,9,1]{0,1,2:T(8,128)(2,1)} %param.21) | copy-start | bytes 1732
  0.0 26.9 %copy-start.3 = (bf16[32,9,32]{2,0,1:T(8,128)(2,1)S(1)}, bf16[32,9,32]{2,0,1:T(8,128)(2,1)}, u32[]{:S(2)}) copy-start(bf16[32,9,32]{2,0,1:T(8,128)(2,1)} %param.22) | copy-start | bytes 55300
  0.0 26.9 %copy-start.1 = (bf16[64,9,32]{0,2,1:T(8,128)(2,1)S(1)}, bf16[64,9,32]{0,2,1:T(8,128)(2,1)}, u32[]{:S(2)}) copy-start(bf16[64,9,32]{0,2,1:T(8,128)(2,1)} %param.23) | copy-start | bytes 110596
  0.0 26.9 %copy-start = (bf16[64,9,64]{2,0,1:T(8,128)(2,1)S(1)}, bf16[64,9,64]{2,0,1:T(8,128)(2,1)}, u32[]{:S(2)}) copy-start(bf16[64,9,64]{2,0,1:T(8,128)(2,1)} %param.24) | copy-start | bytes 221188
  0.0 26.9 %copy-start.4 = (bf16[32,9,96]{2,0,1:T(8,128)(2,1)S(1)}, bf16[32,9,96]{2,0,1:T(8,128)(2,1)}, u32[]{:S(2)}) copy-start(bf16[32,9,96]{2,0,1:T(8,128)(2,1)} %param.25) | copy-start | bytes 165892
  0.0 26.9 %copy-start.2 = (bf16[32,9,32]{2,0,1:T(8,128)(2,1)S(1)}, bf16[32,9,32]{2,0,1:T(8,128)(2,1)}, u32[]{:S(2)}) copy-start(bf16[32,9,32]{2,0,1:T(8,128)(2,1)} %param.26) | copy-start | bytes 55300
  0.0 26.9 %copy-start.6 = (bf16[32]{0:T(256)(128)(2,1)S(1)}, bf16[32]{0:T(256)(128)(2,1)}, u32[]{:S(2)}) copy-start(bf16[32]{0:T(256)(128)(2,1)} %param.27) | copy-start | bytes 196
  2.0 7.4 %all-to-all-start.2 = ((bf16[2,2,8192]{2,1,0:T(2,128)(2,1)}), bf16[2,2,8192]{2,1,0:T(2,128)(2,1)S(1)}, u32[]{:S(2)}, u32[]{:S(2)}) async-start(bf16[2,2,8192]{2,1,0:T(2,128)(2,1)} %reshape.146), calls=%async_computation.2 | async-start | bytes 131072 | tf_op jit(solution)/shard_map/all_to_all | solution.py:97
  9.4 7.4 %all-to-all-start = ((bf16[2,16,1024]{2,0,1:T(2,128)(2,1)}), bf16[2,16,1024]{2,0,1:T(2,128)(2,1)S(1)}, u32[]{:S(2)}, u32[]{:S(2)}) async-start(bf16[2,16,1024]{2,0,1:T(2,128)(2,1)} %copy.769), calls=%async_computation | async-start | bytes 131072 | tf_op jit(solution)/shard_map/all_to_all | solution.py:85
  16.8 9.7 %all-to-all-start.3 = ((bf16[8,2,2048]{2,1,0:T(2,128)(2,1)}), bf16[8,2,2048]{2,1,0:T(2,128)(2,1)S(1)}, u32[]{:S(2)}, u32[]{:S(2)}) async-start(bf16[8,2,2048]{2,1,0:T(2,128)(2,1)} %reshape.148), calls=%async_computation.3 | async-start | bytes 131072 | tf_op jit(solution)/shard_map/all_to_all | solution.py:96
  159.6 7.4 %all-to-all-start.4 = ((bf16[2,2,8192]{2,1,0:T(2,128)(2,1)}), bf16[2,2,8192]{2,1,0:T(2,128)(2,1)S(1)}, u32[]{:S(2)}, u32[]{:S(2)}) async-start(bf16[2,2,8192]{2,1,0:T(2,128)(2,1)} %reshape.150), calls=%async_computation.4 | async-start | bytes 131072 | tf_op jit(solution)/shard_map/all_to_all | solution.py:111
  168.0 84.8 %all-to-all-start.5 = ((bf16[8,2,2048]{2,1,0:T(2,128)(2,1)}), bf16[8,2,2048]{2,1,0:T(2,128)(2,1)S(1)}, u32[]{:S(2)}, u32[]{:S(2)}) async-start(bf16[8,2,2048]{2,1,0:T(2,128)(2,1)} %reshape.152), calls=%async_computation.5 | async-start | bytes 131072 | tf_op jit(solution)/shard_map/all_to_all | solution.py:110
  252.8 7.4 %all-to-all-start.1 = ((bf16[4,8,1024]{2,1,0:T(8,128)(2,1)}), bf16[4,8,1024]{2,1,0:T(8,128)(2,1)S(1)}, u32[]{:S(2)}, u32[]{:S(2)}) async-start(bf16[4,8,1024]{2,1,0:T(8,128)(2,1)} %copy.771), calls=%async_computation.1 | async-start | bytes 131072 | tf_op jit(solution)/shard_map/all_to_all | solution.py:90
where the time goes:
time: 257 us; the launch traced here: 261 us
  local copies, waits for them, and re-layouts  109 us (42%)
  starting transfers between devices  47.5 us (18%)
  matrix products  33.8 us (13%)
  loops' own time  30 us (12%)
  waiting for transfers between devices  15.6 us (6%)
  blocking collectives  14.6 us (6%)
  other arithmetic  10.5 us (4%)
    cond x722, local copies, waits for them, and re-layouts  50.9 us
    all_to_all x1, starting transfers between devices, per_device(): lax.all_to_all(lax.all_to_all(yz_grid, 'slab', split_axis=2, concat_axis=...  28.2 us
    dot_general x95, matrix products, convolve(): jnp.einsum('ok,khw->ohw', matrix, stacked, preferred_element_type=jnp.flo...  26.6 us
    another operation x2, loops' own time, restore(): finished = lax.map(single, (own_planes, own_tissue))  24.6 us
    dynamic_slice x36, local copies, waits for them, and re-layouts, restore(): finished = lax.map(single, (own_planes, own_tissue))  21.3 us
    all_gather x2, blocking collectives, restore(): return lax.all_gather(finished, 'ch', axis=0, tiled=True)  14.6 us
    another operation x304, local copies, waits for them, and re-layouts, convolve(): jnp.stack([padded[:, row_shift:row_shift + height, col_shift:col_shift +...  13.7 us
    reduce_sum x19, other arithmetic, shrink(): return jnp.mean(blocks, axis=(2, 4)).astype(jnp.bfloat16)  8.45 us
  transfers between devices with their start and end apart: 6, of which 5 were waited for; matrix products, arithmetic and copies ran while one was open for 17% of the time, Pallas kernels for 0%

commit v1 on v0

v1 whole, which is shorter than its diff:
```python
import functools

import jax
import jax.numpy as jnp
from jax import lax
from jax.experimental import pallas as pl
from jax.experimental.pallas import tpu as pltpu
from jax.sharding import PartitionSpec as P

MESH = pl.DeviceIdType.MESH
HALO = 8
GROUP = 64
BLOCK = 16
BF = jnp.bfloat16
F32 = jnp.float32


def iota(shape, axis):
    return lax.broadcasted_iota(jnp.int32, shape, axis)


def dot(a, b):
    return jnp.dot(a, b, preferred_element_type=F32)


def spread(wide, taps):
    count, outs = taps.shape
    lanes = wide.shape[1]
    repeat = jnp.where(iota((outs, lanes), 1) % outs == iota((outs, lanes), 0), 1.0, 0.0)
    wide[0:count, :] = dot(taps, repeat.astype(BF))


def band(dst, row, wide, depth, first, count, lanes, half, outs, pick):
    lane = iota((1, lanes), 1)
    p, zo = lane // half, (lane % half) // outs
    total = jnp.zeros((count, lanes), F32)
    for r in range(3):
        for s in range(3):
            hit = pick(p, zo, r, s)
            if hit is None:
                continue
            start = (3 * r + s) * depth + first
            total = total + jnp.where(hit, wide[start : start + count, :], 0.0)
    dst[row : row + count, :] = total.astype(BF)


def plain_pick(q, zi):
    def pick(p, zo, r, s):
        if s not in (q, q - 1):
            return None
        return (p == q - s) & (zo == zi + 1 - r)

    return pick


def up_pick(d, zp, levels):
    def pick(p, zo, r, s):
        z = zo + r - 1
        return ((p + s + 1) // 2 - 1 == d) & (z >= 0) & (z < levels) & (z // 2 == zp)

    return pick


def kernel(
    slabs, tiles, chs,
    vol, xz_flag, yz_flag, k1, k2, k3, k4, k5, k6, tail,
    out,
    vxz, ryz, turned, w1, w2, w3, w4, w5, w6,
    e1, e2, pooled, m1, m2, wide,
    xr, yt, place, rx, ry,
    in_local, xin_send, xin_recv, yin_send, yin_recv,
    xo_send, xo_recv, yo_send, yo_recv,
):
    d1, d2 = e1, e2
    zd, yd, across = vol.shape
    levels = slabs * zd
    breadth = tiles * yd
    devices = slabs * tiles * chs
    half = 32 * levels
    full = 2 * half
    small = half <= 128
    window = 4 * levels
    per_chunk = 128 // window
    width = across // (slabs * chs)
    cols = across // devices
    rows_y = max(16, cols)
    s, t, c = lax.axis_index("slab"), lax.axis_index("tile"), lax.axis_index("ch")
    g = s * chs + c
    me = (s * tiles + t) * chs + c

    def coords(k):
        return k // (tiles * chs), (k // chs) % tiles, k % chs

    def others(body):
        def step(k, carry):
            @pl.when(k != me)
            def _():
                body(k)

            return carry

        lax.fori_loop(0, devices, step, 0)

    barrier = pltpu.get_barrier_semaphore()

    def greet(k):
        ks, kt, kc = coords(k)
        pl.semaphore_signal(
            barrier, inc=1, device_id={"slab": ks, "tile": kt, "ch": kc}, device_id_type=MESH
        )

    others(greet)
    pl.semaphore_wait(barrier, devices - 1)

    def xin(k):
        return pltpu.make_async_remote_copy(
            src_ref=vol,
            dst_ref=vxz.at[pl.ds(s * zd, zd), :, pl.ds(128, across)],
            send_sem=xin_send.at[k],
            recv_sem=xin_recv.at[s],
            device_id={"slab": k, "tile": t, "ch": c},
            device_id_type=MESH,
        )

    def xin_from(k):
        return pltpu.make_async_remote_copy(
            src_ref=vol,
            dst_ref=vxz.at[pl.ds(k * zd, zd), :, pl.ds(128, across)],
            send_sem=xin_send.at[k],
            recv_sem=xin_recv.at[k],
            device_id={"slab": k, "tile": t, "ch": c},
            device_id_type=MESH,
        )

    def lanes_of(k):
        return pl.ds(pl.multiple_of((k * cols * chs) // 128 * 128, 128), 128)

    def yin(k):
        ks, kt = k // tiles, k % tiles
        return pltpu.make_async_remote_copy(
            src_ref=vol.at[:, :, lanes_of(k)],
            dst_ref=ryz.at[t, s],
            send_sem=yin_send.at[k],
            recv_sem=yin_recv.at[s * tiles + t],
            device_id={"slab": ks, "tile": kt, "ch": c},
            device_id_type=MESH,
        )

    def yin_from(k):
        ks, kt = k // tiles, k % tiles
        return pltpu.make_async_remote_copy(
            src_ref=vol.at[:, :, lanes_of(k)],
            dst_ref=ryz.at[kt, ks],
            send_sem=yin_send.at[k],
            recv_sem=yin_recv.at[k],
            device_id={"slab": ks, "tile": kt, "ch": c},
            device_id_type=MESH,
        )

    def loop(count, own, body):
        def step(k, carry):
            @pl.when(k != own)
            def _():
                body(k)

            return carry

        lax.fori_loop(0, count, step, 0)

    place_me = s * tiles + t
    loop(slabs, s, lambda k: xin(k).start())
    loop(slabs * tiles, place_me, lambda k: yin(k).start())
    own_x = pltpu.make_async_copy(
        vol, vxz.at[pl.ds(s * zd, zd), :, pl.ds(128, across)], in_local.at[0]
    )
    own_y = pltpu.make_async_copy(vol.at[:, :, lanes_of(place_me)], ryz.at[t, s], in_local.at[1])
    own_x.start()
    own_y.start()

    edge = jnp.zeros((levels, yd, 128), BF)
    vxz[:, :, 0:128] = edge
    vxz[:, :, 128 + across :] = edge

    spread(wide, k1[...])
    line, lane = iota((window, full), 0), iota((window, full), 1)
    base = jnp.zeros((window, full), F32)
    for r in range(3):
        for q in range(3):
            hit = (line // levels - lane // half == q) & (
                line % levels - (lane % half) // 32 + 1 == r
            )
            base = base + jnp.where(hit, wide[3 * r + q : 3 * r + q + 1, :], 0.0)
    base = base.astype(BF)
    w1[...] = jnp.zeros(w1.shape, BF)
    for m in range(per_chunk):
        w1[m * window : (m + 1) * window, m * full : (m + 1) * full] = base

    order = (1, 2, 0, 3)
    for kk, ww in ((k2, w2), (k6, w6)):
        spread(wide, kk[...])
        for n, q in enumerate(order):
            for zi in range(levels):
                band(ww, n * half + 32 * zi, wide, 32, 0, 32, full, half, 32, plain_pick(q, zi))
    spread(wide, k3[...])
    for n, q in enumerate(order):
        for zi in range(levels // 2):
            band(w3, n * half + 64 * zi, wide, 32, 0, 32, full, half, 64, plain_pick(q, zi))
            w3[n * half + 64 * zi + 32 : n * half + 64 * zi + 64, :] = jnp.zeros((32, full), BF)
    spread(wide, k4[...])
    for n, q in enumerate(order):
        for zi in range(levels // 2):
            band(w4, n * half + 64 * zi, wide, 64, 0, 64, full, half, 64, plain_pick(q, zi))
    spread(wide, k5[...])
    for n, q in enumerate(order):
        for zi in range(levels):
            band(w5, n * half + 32 * zi, wide, 96, 64, 32, full, half, 32, plain_pick(q, zi))
    for n, d in enumerate((-1, 0, 1)):
        for zp in range(levels // 2):
            band(
                w5, (4 + n) * half + 64 * zp, wide, 96, 0, 64, full, half, 32,
                up_pick(d, zp, levels),
            )

    def pieces(count, rows):
        best = 1
        for n in range(1, count + 1):
            if count % n == 0 and count // n * rows * half >= 384 * 128:
                best = n
        return best

    def ranged(lo, hi, rows, body):
        n = pieces(hi - lo, rows)
        size = (hi - lo) // n
        for i in range(n):
            body(lo + i * size, size)

    def around(src, a, n):
        return [
            src[a + 1 : a + 1 + n],
            src[a : a + n][:, :, half:],
            src[a + 2 : a + 2 + n][:, :, :half],
        ]

    def conv(parts, weight, n, rows):
        joined = jnp.concatenate(parts, axis=-1)
        joined = joined.reshape(n * rows, joined.shape[-1])
        return jnp.maximum(dot(joined, weight[...]), 0.0).astype(BF).reshape(n, rows, full)

    def network(u, rows, pairs, margin, clear):
        chunks = pairs // per_chunk
        for ref in (e1, e2):
            z1 = jnp.zeros((1, rows, full), BF)
            ref[0:1, 0:rows] = z1
            ref[pairs + 1 : pairs + 2, 0:rows] = z1
        for ref in (pooled, m1):
            z1 = jnp.zeros((1, rows, full), BF)
            ref[0:1, 0:rows] = z1
            ref[pairs // 2 + 1 : pairs // 2 + 2, 0:rows] = z1
        z1 = jnp.zeros((1, rows, half), BF)
        m2[0:1, 0:rows] = z1
        m2[pairs + 1 : pairs + 2, 0:rows] = z1
        flat = u.reshape(chunks * rows, 128)
        for m in range(per_chunk):
            got = jnp.maximum(dot(flat, w1[:, m * full : (m + 1) * full]), 0.0).astype(BF)
            got = got.reshape(chunks, rows, full)
            for i in range(chunks):
                e1[i * per_chunk + m + 1, 0:rows] = got[i]
        clear(e1)
        need = margin // 2

        def second(a, n):
            parts = [x[:, 0:rows] for x in around(e1, a, n)]
            got = conv(parts, w2, n, rows)
            e2[a + 1 : a + 1 + n, 0:rows] = got

        ranged(need, pairs - need, rows, second)
        clear(e2)

        def shrink(a, n):
            x = e2[2 * a + 1 : 2 * a + 1 + 2 * n, 0:rows].astype(F32)
            x = (x[:, :, :half] + x[:, :, half:]).reshape(2 * n * rows, half)
            x = (x + pltpu.roll(x, half - 32, axis=1)) * 0.25
            x = x.astype(BF).reshape(n, 2, rows, half)
            pooled[a + 1 : a + 1 + n, 0:rows] = jnp.concatenate([x[:, 0], x[:, 1]], axis=-1)

        ranged(need // 2, pairs // 2 - need // 2, rows, shrink)

        def third(a, n):
            parts = [x[:, 0:rows] for x in around(pooled, a, n)]
            m1[a + 1 : a + 1 + n, 0:rows] = conv(parts, w3, n, rows)

        ranged(need // 2, pairs // 2 - need // 2, rows, third)
        clear(m1, 2)

        def fourth(a, n):
            parts = [x[:, 0:rows] for x in around(m1, a, n)]
            got = conv(parts, w4, n, rows)
            for i in range(n):
                m2[2 * (a + i) + 1, 0:rows] = got[i, :, :half]
                m2[2 * (a + i) + 2, 0:rows] = got[i, :, half:]

        ranged(need // 2, pairs // 2 - need // 2, rows, fourth)
        clear(m2)

        def fifth(a, n):
            parts = [x[:, 0:rows] for x in around(e2, a, n)]
            parts += [m2[a + i : a + i + n, 0:rows] for i in range(3)]
            d1[a + 1 : a + 1 + n, 0:rows] = conv(parts, w5, n, rows)

        ranged(need, pairs - need, rows, fifth)
        clear(d1)

        def sixth(a, n):
            parts = [x[:, 0:rows] for x in around(d1, a, n)]
            d2[a - margin : a - margin + n, 0:rows] = conv(parts, w6, n, rows)

        ranged(margin, pairs - margin, rows, sixth)

        inner = pairs - 2 * margin
        blocks = inner // BLOCK
        line, lane = iota((full, half), 0), iota((full, half), 1)
        aim = (line % half) // 32 * 32 + line // half

        def add(m, head):
            weight = jnp.where(lane == aim + 2 * m, tail[...].astype(F32), 0.0).astype(BF)
            x = jnp.concatenate([d2[b * BLOCK + m, 0:rows] for b in range(blocks)], axis=0)
            return head + dot(x, weight)

        zero = jnp.zeros((blocks * rows, half), F32)
        head = lax.fori_loop(0, BLOCK, add, zero, unroll=small)
        parts_per = BLOCK // per_chunk
        first = margin // per_chunk
        line, lane = iota((128, half), 0), iota((128, half), 1)
        pair, q, z = line // window, (line % window) // levels, line % levels
        picture = jnp.zeros((blocks * rows, half), F32)
        for i in range(parts_per):
            hit = (q > 0) & (q < 3) & (lane == z * 32 + 2 * (i * per_chunk + pair) + q - 1)
            pickout = jnp.where(hit, 1.0, 0.0).astype(BF)
            x = jnp.concatenate([u[first + b * parts_per + i] for b in range(blocks)], axis=0)
            picture = picture + dot(x, pickout)
        return head, picture, blocks

    def windows(source, deep, rows, pairs, offset):
        strip = min(pairs * window, 1024)
        lane, col = iota((deep, strip), 0), iota((deep, strip), 1)
        ahead = lane - offset - 2 * (col // window) - (col % window) // levels
        chunks = []
        for start in range(0, pairs * window, strip):

            def add(z, total, start=start):
                hit = (ahead == 2 * (start // window)) & (col % levels == z)
                return total + dot(source(z), jnp.where(hit, 1.0, 0.0).astype(BF))

            zero = jnp.zeros((rows, strip), F32)
            total = lax.fori_loop(0, levels, add, zero, unroll=small)
            total = total.astype(BF)
            chunks += [total[:, i : i + 128] for i in range(0, strip, 128)]
        return chunks

    own_x.wait()
    loop(slabs, s, lambda k: xin_from(k).wait_recv())
    pairs_x = width // 2 + 2 * HALO
    groups = -(-pairs_x // GROUP)
    lead = 128 + g * width - 2 * HALO - 1
    base_lane = lead // 128 * 128

    def x_source(z):
        return jnp.concatenate(
            [
                vxz[z, :, pl.ds(pl.multiple_of(base_lane + 128 * n, 128), 256)]
                for n in range(groups)
            ],
            axis=0,
        )

    chunk_list = windows(x_source, 256, groups * yd, GROUP, lead - base_lane)
    u = [x[n * yd : (n + 1) * yd] for n in range(groups) for x in chunk_list]
    u = jnp.stack(u[: pairs_x // per_chunk])

    def clear(ref, by=1):
        h, n = HALO // by, pairs_x // by
        zero = jnp.zeros((h, yd, ref.shape[-1]), BF)

        @pl.when(g == 0)
        def _():
            ref[1 : 1 + h, 0:yd] = zero

        @pl.when(g == slabs * chs - 1)
        def _():
            ref[1 + n - h : 1 + n, 0:yd] = zero

    head, picture, blocks = network(u, yd, pairs_x, HALO, clear)
    flag = jnp.concatenate([xz_flag[...]] * blocks, axis=0)
    done = jnp.where(flag[:, 0:1] > 0, picture + head, picture).astype(BF)
    done = done.reshape(blocks, yd, half)
    span = xr.shape[-1]
    per = min(4, blocks)
    skew = lax.rem(g * width, 128)
    line, lane = iota((half, levels * 128), 0), iota((half, levels * 128), 1)
    for n in range(span // 128):
        total = jnp.zeros((yd, levels * 128), F32)
        for b in range(per):
            hit = lane == line // 32 * 128 + skew + 32 * b + line % 32
            total = total + dot(done[n * per + b], jnp.where(hit, 1.0, 0.0).astype(BF))
        total = total.astype(BF)
        for z in range(levels):
            xr[z, :, 128 * n : 128 * (n + 1)] = total[:, 128 * z : 128 * (z + 1)]

    def xo(k):
        return pltpu.make_async_remote_copy(
            src_ref=xr.at[pl.ds(k // chs * zd, zd)],
            dst_ref=rx.at[g],
            send_sem=xo_send.at[k],
            recv_sem=xo_recv.at[g],
            device_id={"slab": k // chs, "tile": t, "ch": k % chs},
            device_id_type=MESH,
        )

    def xo_from(k):
        return pltpu.make_async_remote_copy(
            src_ref=xr.at[pl.ds(k // chs * zd, zd)],
            dst_ref=rx.at[k],
            send_sem=xo_send.at[k],
            recv_sem=xo_recv.at[k],
            device_id={"slab": k // chs, "tile": t, "ch": k % chs},
            device_id_type=MESH,
        )

    loop(slabs * chs, g, lambda k: xo(k).start())
    own_xo = pltpu.make_async_copy(xr.at[pl.ds(s * zd, zd)], rx.at[g], in_local.at[2])
    own_xo.start()

    own_y.wait()
    loop(slabs * tiles, place_me, lambda k: yin_from(k).wait_recv())
    for z in range(levels):
        plane = ryz[:, z // zd, z % zd].reshape(breadth, 128).astype(F32)
        turned[z] = plane.T
    in_block = lax.rem(me * cols, 128)
    row_start = pl.multiple_of(in_block // rows_y * rows_y, rows_y)

    def y_source(z):
        return turned[z, pl.ds(row_start, rows_y), :].astype(BF)

    pairs_y = breadth // 2
    u = jnp.stack(windows(y_source, breadth, rows_y, pairs_y, -1))
    head, picture, blocks = network(u, rows_y, pairs_y, 0, lambda ref, by=1: None)
    row = iota((rows_y, 1), 0) + row_start
    mine = (row >= in_block) & (row < in_block + cols)
    flag = yz_flag[pl.ds(row_start, rows_y), 0:1]
    for b in range(blocks):
        a = slice(b * rows_y, (b + 1) * rows_y)
        got = jnp.where(flag > 0, picture[a] + head[a], picture[a])
        place[...] = jnp.zeros(place.shape, F32)
        place[pl.ds(row_start, rows_y), :] = jnp.where(mine, got, 0.0)
        yt[b] = place[...].T.astype(BF).reshape(levels, 32 // yd, yd, 128)

    fold = 32 // yd

    def yo(k):
        ks, kt, kc = coords(k)
        return pltpu.make_async_remote_copy(
            src_ref=yt.at[kt // fold, pl.ds(ks * zd, zd), lax.rem(kt, fold)],
            dst_ref=ry.at[me],
            send_sem=yo_send.at[k],
            recv_sem=yo_recv.at[me],
            device_id={"slab": ks, "tile": kt, "ch": kc},
            device_id_type=MESH,
        )

    def yo_from(k):
        ks, kt, kc = coords(k)
        return pltpu.make_async_remote_copy(
            src_ref=yt.at[kt // fold, pl.ds(ks * zd, zd), lax.rem(kt, fold)],
            dst_ref=ry.at[k],
            send_sem=yo_send.at[k],
            recv_sem=yo_recv.at[k],
            device_id={"slab": ks, "tile": kt, "ch": kc},
            device_id_type=MESH,
        )

    others(lambda k: yo(k).start())
    own_yo = pltpu.make_async_copy(
        yt.at[t // fold, pl.ds(s * zd, zd), lax.rem(t, fold)], ry.at[me], in_local.at[3]
    )
    own_yo.start()
    own_xo.wait()
    loop(slabs * chs, g, lambda k: xo_from(k).wait_recv())
    own_yo.wait()
    others(lambda k: yo_from(k).wait_recv())
    for b in range(across // 128):
        if width >= 128:
            at = b * 128 % width
            xz = rx[b * 128 // width, :, :, at : at + 128].astype(F32)
        else:
            each = 128 // width
            xz = sum(rx[b * each + i].astype(F32) for i in range(each))
        each = 128 // cols
        yz = sum(ry[b * each + i].astype(F32) for i in range(each))
        out[:, :, 128 * b : 128 * (b + 1)] = (0.5 * (xz + yz)).astype(BF)
    loop(slabs, s, lambda k: xin(k).wait_send())
    loop(slabs * tiles, place_me, lambda k: yin(k).wait_send())
    loop(slabs * chs, g, lambda k: xo(k).wait_send())
    others(lambda k: yo(k).wait_send())


def taps_first(weight):
    return jnp.transpose(weight, (1, 2, 0)).reshape(-1, weight.shape[0])


def per_device(
    volume, xz_tissue, yz_tissue,
    first_conv, second_conv, third_conv, fourth_conv, fifth_conv, sixth_conv, out_weight,
):
    slabs, tiles, chs = (lax.axis_size(name) for name in ("slab", "tile", "ch"))
    zd, yd, across = volume.shape
    levels, breadth = slabs * zd, tiles * yd
    devices = slabs * tiles * chs
    half, full = 32 * levels, 64 * levels
    width, cols = across // (slabs * chs), across // devices
    rows_y = max(16, cols)
    rows = max(yd, rows_y)
    most = max(width // 2 + 2 * HALO, breadth // 2)
    span = max(128, width)
    held = cols * chs
    place = lax.axis_index("slab") * tiles + lax.axis_index("tile")
    xz_flag = jnp.broadcast_to(xz_tissue[:, None], (yd, 128))
    spot = lax.rem(place * held, 128)
    yz_flag = lax.dynamic_update_slice(
        jnp.zeros((128,), jnp.int32), yz_tissue, (spot,)
    )
    yz_flag = jnp.broadcast_to(yz_flag[:, None], (128, 128))
    tail = jnp.broadcast_to(jnp.tile(out_weight, 2 * levels)[:, None], (full, half))
    first = jnp.pad(taps_first(first_conv), ((0, 7), (0, 0)))
    dma = pltpu.SemaphoreType.DMA
    vmem = pl.BlockSpec(memory_space=pltpu.VMEM)

    def act(n, lanes, m=rows):
        return pltpu.VMEM((n, m, lanes), BF)

    return pl.pallas_call(
        functools.partial(kernel, slabs, tiles, chs),
        out_shape=jax.ShapeDtypeStruct((zd, yd, across), BF),
        in_specs=[vmem] * 10,
        out_specs=vmem,
        scratch_shapes=[
            pltpu.VMEM((levels, yd, across + 256), BF),
            pltpu.VMEM((tiles, slabs, zd, yd, 128), BF),
            pltpu.VMEM((levels, 128, breadth), F32),
            pltpu.VMEM((128, 128 // (4 * levels) * full), BF),
            pltpu.VMEM((4 * half, full), BF),
            pltpu.VMEM((4 * half, full), BF),
            pltpu.VMEM((4 * half, full), BF),
            pltpu.VMEM((7 * half, full), BF),
            pltpu.VMEM((4 * half, full), BF),
            act(most + 2, full),
            act(most + 2, full),
            act(most // 2 + 2, full),
            act(most // 2 + 2, full),
            act(most + 2, half),
            pltpu.VMEM((9 * 96, full), F32),
            pltpu.VMEM((levels, yd, span), BF),
            pltpu.VMEM((breadth // 32, levels, 32 // yd, yd, 128), BF),
            pltpu.VMEM((128, half), F32),
            pltpu.VMEM((slabs * chs, zd, yd, span), BF),
            pltpu.VMEM((devices, zd, yd, 128), BF),
            dma((4,)),
            dma((slabs,)), dma((slabs,)),
            dma((slabs * tiles,)), dma((slabs * tiles,)),
            dma((slabs * chs,)), dma((slabs * chs,)),
            dma((devices,)), dma((devices,)),
        ],
        compiler_params=pltpu.CompilerParams(
            collective_id=0, has_side_effects=True, vmem_limit_bytes=58 * 1024 * 1024
        ),
    )(
        volume, xz_flag, yz_flag, first,
        taps_first(second_conv), taps_first(third_conv), taps_first(fourth_conv),
        taps_first(fifth_conv), taps_first(sixth_conv), tail,
    )


def solution(mesh):
    return jax.shard_map(
        per_device,
        mesh=mesh,
        in_specs=(P("slab", "tile", None), P("tile"), P(("slab", "tile"))) + (P(),) * 7,
        out_specs=P("slab", "tile", None),
        check_vma=False,
    )
```

time: 257 us -> 37.6 us (0.15)
  the two profiles are of different devices: /device:TPU:24 before, /device:TPU:0 now
where the time goes in v1:
time: 37.6 us; the launch traced here: 37.1 us
  Pallas kernels  28.7 us (76%)
  local copies, waits for them, and re-layouts  8.28 us (22%)
    pallas_call x1, Pallas kernels, per_device(): pl.pallas_call(functools.partial(kernel, slabs, tiles, chs), out_shape=ja...  28.7 us
    transpose x4, local copies, waits for them, and re-layouts, taps_first(): return jnp.transpose(weight, (1, 2, 0)).reshape(-1, weight.shape[0])  3.08 us
    unnamed x17, local copies, waits for them, and re-layouts  2.24 us
    broadcast_in_dim x2, local copies, waits for them, and re-layouts, per_device(): jnp.broadcast_to(jnp.tile(out_weight, 2 * levels)[:, None], (full, half))  0.8 us

profile of v1, /device:TPU:0, one launch (start us, length us, event | category | flops | bytes accessed | tf_op | source)
XLA Modules:
  0.0 37.1 jit_solution(8362867676538585166)
XLA Ops:
  0.0 0.0 copy-start.7
  0.0 0.0 copy-start.5
  0.0 0.0 copy-start.4
  0.0 0.6 %copy-done.7 = s32[64]{0:T(128)S(1)} copy-done((s32[64]{0:T(128)S(1)}, s32[64]{0:T(128)}, u32[]{:S(2)}) %copy-start.7) | copy-done | bytes 280
  0.7 0.2 dynamic_update_slice.5
  0.8 0.0 copy-done.5
  0.8 0.0 copy-start.6
  0.9 0.1 broadcast_in_dim.25
  0.9 0.0 copy-done.4
  0.9 0.6 %pad.4.k1 = bf16[16,32]{1,0:T(8,128)(2,1)} pad(bf16[9,32]{1,0:T(8,128)(2,1)S(1)} %bitcast.23, bf16[]{:T(256)} %constant.25.clone.1), padding=0_7x0_0 | pad | bytes 1602 | tf_op jit(solution)/shard_map/jit(_pad)/pad | solution.py:533
  1.5 0.0 copy-done.6
  1.5 0.7 %broadcast_in_dim.10.xz_flag = s32[16,128]{1,0:T(8,128)} broadcast(s32[16]{0:T(128)S(1)} %copy-done.6), dimensions={0} | broadcast | bytes 8256 | tf_op jit(solution)/shard_map/broadcast_in_dim | solution.py:526
  2.2 0.7 %broadcast_in_dim.26.tail = bf16[256,128]{1,0:T(8,128)(2,1)} broadcast(bf16[256]{0:T(256)(128)(2,1)S(1)} %broadcast_in_dim.25), dimensions={0} | broadcast | bytes 66048 | tf_op jit(solution)/shard_map/broadcast_in_dim | solution.py:532
  2.9 0.7 %broadcast_in_dim.24.yz_flag = s32[128,128]{1,0:T(8,128)} broadcast(s32[128]{0:T(128)S(1)} %dynamic_update_slice.5), dimensions={0} | broadcast | bytes 66048 | tf_op jit(solution)/shard_map/broadcast_in_dim | solution.py:531
  3.6 0.0 copy-done.1
  3.6 0.7 %copy.11 = bf16[9,32,32]{2,1,0:T(8,128)(2,1)} copy(bf16[9,32,32]{1,2,0:T(8,128)(2,1)S(1)} %bitcast.19) | data formatting | bytes 36864 | tf_op jit(solution)/shard_map/transpose | solution.py:507
  4.4 0.0 copy-done.2
  4.4 0.7 %copy.14 = bf16[9,32,32]{2,1,0:T(8,128)(2,1)} copy(bf16[9,32,32]{1,2,0:T(8,128)(2,1)S(1)} %bitcast.20) | data formatting | bytes 36864 | tf_op jit(solution)/shard_map/transpose | solution.py:507
  5.1 0.0 copy-done
  5.1 0.8 %copy.12 = bf16[9,64,64]{2,1,0:T(8,128)(2,1)} copy(bf16[9,64,64]{1,2,0:T(8,128)(2,1)S(1)} %bitcast.18) | data formatting | bytes 147456 | tf_op jit(solution)/shard_map/transpose | solution.py:507
  5.9 0.1 copy-done.3
  6.0 0.8 %copy.13 = bf16[9,96,32]{2,1,0:T(8,128)(2,1)} copy(bf16[9,96,32]{1,2,0:T(8,128)(2,1)S(1)} %bitcast.21) | data formatting | bytes 110592 | tf_op jit(solution)/shard_map/transpose | solution.py:507
  6.8 28.7 %shard_map.100 = bf16[2,16,1024]{2,1,0:T(8,128)(2,1)} custom-call(bf16[2,16,1024]{2,1,0:T(8,128)(2,1)} %vol.1, s32[16,128]{1,0:T(8,128)} %broadcast_in_dim.10.xz_flag, s32[128,128]{1,0:T(8,128)} %broadcast_in_dim.24.yz_flag, bf16[16,32]{1,0:T(8,128)(2,1)} %pad.4.k1, bf16[288,32]{1,0:T(8,128)(2,1)} %bitcast.16, bf16[288,64]{1,0:T(8,128)(2,1)} %bitcast.22, ...), custom_call_target="tpu_custom_call" | custom-call | tf_op jit(solution)/shard_map/pallas_call | solution.py:540
  35.6 1.5 %copy.17 = bf16[2,16,1024]{2,1,0:T(8,128)(2,1)} copy(bf16[2,16,1024]{2,1,0:T(8,128)(2,1)} %shard_map.100) | data formatting | bytes 131072
  (6 shorter events, 0.0 us)
Async XLA Ops:
  0.0 0.7 %copy-start.7 = (s32[64]{0:T(128)S(1)}, s32[64]{0:T(128)}, u32[]{:S(2)}) copy-start(s32[64]{0:T(128)} %param.12) | copy-start | bytes 772
  0.0 0.8 %copy-start.5 = (bf16[32]{0:T(256)(128)(2,1)S(1)}, bf16[32]{0:T(256)(128)(2,1)}, u32[]{:S(2)}) copy-start(bf16[32]{0:T(256)(128)(2,1)} %param.19) | copy-start | bytes 196
  0.0 0.9 %copy-start.4 = (bf16[32,9,1]{0,1,2:T(8,128)(2,1)S(1)}, bf16[32,9,1]{0,1,2:T(8,128)(2,1)}, u32[]{:S(2)}) copy-start(bf16[32,9,1]{0,1,2:T(8,128)(2,1)} %param.13) | copy-start | bytes 1732
  0.8 0.7 %copy-start.6 = (s32[16]{0:T(128)S(1)}, s32[16]{0:T(128)}, u32[]{:S(2)}) copy-start(s32[16]{0:T(128)} %param.11) | copy-start | bytes 196
  0.9 2.7 %copy-start.1 = (bf16[32,9,32]{2,0,1:T(8,128)(2,1)S(1)}, bf16[32,9,32]{2,0,1:T(8,128)(2,1)}, u32[]{:S(2)}) copy-start(bf16[32,9,32]{2,0,1:T(8,128)(2,1)} %param.14) | copy-start | bytes 55300
  2.9 1.4 %copy-start.2 = (bf16[32,9,32]{2,0,1:T(8,128)(2,1)S(1)}, bf16[32,9,32]{2,0,1:T(8,128)(2,1)}, u32[]{:S(2)}) copy-start(bf16[32,9,32]{2,0,1:T(8,128)(2,1)} %param.18) | copy-start | bytes 55300
  3.6 1.5 %copy-start = (bf16[64,9,64]{2,0,1:T(8,128)(2,1)S(1)}, bf16[64,9,64]{2,0,1:T(8,128)(2,1)}, u32[]{:S(2)}) copy-start(bf16[64,9,64]{2,0,1:T(8,128)(2,1)} %param.16) | copy-start | bytes 221188
  5.1 0.9 %copy-start.3 = (bf16[32,9,96]{2,0,1:T(8,128)(2,1)S(1)}, bf16[32,9,96]{2,0,1:T(8,128)(2,1)}, u32[]{:S(2)}) copy-start(bf16[32,9,96]{2,0,1:T(8,128)(2,1)} %param.17) | copy-start | bytes 165892

commit v2 on v1

--- a/solution.py
+++ b/solution.py
@@ -30,17 +30,17 @@
     wide[0:count, :] = dot(taps, repeat.astype(BF))
 
 
-def band(dst, row, wide, depth, first, count, lanes, half, outs, pick):
-    lane = iota((1, lanes), 1)
-    p, zo = lane // half, (lane % half) // outs
-    total = jnp.zeros((count, lanes), F32)
+def band(dst, row, wide, depth, first, count, spots, pick, disjoint=True):
+    p, zo = spots
+    total = jnp.zeros((count, wide.shape[1]), F32)
     for r in range(3):
         for s in range(3):
             hit = pick(p, zo, r, s)
             if hit is None:
                 continue
             start = (3 * r + s) * depth + first
-            total = total + jnp.where(hit, wide[start : start + count, :], 0.0)
+            tap = wide[start : start + count, :]
+            total = jnp.where(hit, tap if disjoint else total + tap, total)
     dst[row : row + count, :] = total.astype(BF)
 
 
@@ -53,10 +53,9 @@
     return pick
 
 
-def up_pick(d, zp, levels):
+def up_pick(d, zp):
     def pick(p, zo, r, s):
-        z = zo + r - 1
-        return ((p + s + 1) // 2 - 1 == d) & (z >= 0) & (z < levels) & (z // 2 == zp)
+        return ((p + s + 1) >> 1 == d + 1) & ((zo + r - 1) >> 1 == zp)
 
     return pick
 
@@ -89,17 +88,17 @@
     me = (s * tiles + t) * chs + c
 
     def coords(k):
-        return k // (tiles * chs), (k // chs) % tiles, k % chs
+        return lax.div(k, tiles * chs), lax.rem(lax.div(k, chs), tiles), lax.rem(k, chs)
+
+    def loop(count, own, body):
+        def step(i, carry):
+            body(lax.rem(own + i, count))
+            return carry
+
+        lax.fori_loop(1, count, step, 0)
 
     def others(body):
-        def step(k, carry):
-            @pl.when(k != me)
-            def _():
-                body(k)
-
-            return carry
-
-        lax.fori_loop(0, devices, step, 0)
+        loop(devices, me, body)
 
     barrier = pltpu.get_barrier_semaphore()
 
@@ -133,10 +132,10 @@
         )
 
     def lanes_of(k):
-        return pl.ds(pl.multiple_of((k * cols * chs) // 128 * 128, 128), 128)
+        return pl.ds(pl.multiple_of(lax.div(k * cols * chs, 128) * 128, 128), 128)
 
     def yin(k):
-        ks, kt = k // tiles, k % tiles
+        ks, kt = lax.div(k, tiles), lax.rem(k, tiles)
         return pltpu.make_async_remote_copy(
             src_ref=vol.at[:, :, lanes_of(k)],
             dst_ref=ryz.at[t, s],
@@ -147,7 +146,7 @@
         )
 
     def yin_from(k):
-        ks, kt = k // tiles, k % tiles
+        ks, kt = lax.div(k, tiles), lax.rem(k, tiles)
         return pltpu.make_async_remote_copy(
             src_ref=vol.at[:, :, lanes_of(k)],
             dst_ref=ryz.at[kt, ks],
@@ -156,16 +155,6 @@
             device_id={"slab": ks, "tile": kt, "ch": c},
             device_id_type=MESH,
         )
-
-    def loop(count, own, body):
-        def step(k, carry):
-            @pl.when(k != own)
-            def _():
-                body(k)
-
-            return carry
-
-        lax.fori_loop(0, count, step, 0)
 
     place_me = s * tiles + t
     loop(slabs, s, lambda k: xin(k).start())
@@ -182,14 +171,16 @@
     vxz[:, :, 128 + across :] = edge
 
     spread(wide, k1[...])
-    line, lane = iota((window, full), 0), iota((window, full), 1)
+    lane, line = iota((1, full), 1), iota((window, 1), 0)
+    side = lane // half
+    fine = (side, (lane % half) // 32)
+    coarse = (side, (lane % half) // 64)
+    step, level = line // levels, line % levels
     base = jnp.zeros((window, full), F32)
     for r in range(3):
         for q in range(3):
-            hit = (line // levels - lane // half == q) & (
-                line % levels - (lane % half) // 32 + 1 == r
-            )
-            base = base + jnp.where(hit, wide[3 * r + q : 3 * r + q + 1, :], 0.0)
+            hit = (step - side == q) & (level - fine[1] + 1 == r)
+            base = jnp.where(hit, wide[3 * r + q : 3 * r + q + 1, :], base)
     base = base.astype(BF)
     w1[...] = jnp.zeros(w1.shape, BF)
     for m in range(per_chunk):
@@ -200,25 +191,25 @@
         spread(wide, kk[...])
         for n, q in enumerate(order):
             for zi in range(levels):
-                band(ww, n * half + 32 * zi, wide, 32, 0, 32, full, half, 32, plain_pick(q, zi))
+                band(ww, n * half + 32 * zi, wide, 32, 0, 32, fine, plain_pick(q, zi))
     spread(wide, k3[...])
     for n, q in enumerate(order):
         for zi in range(levels // 2):
-            band(w3, n * half + 64 * zi, wide, 32, 0, 32, full, half, 64, plain_pick(q, zi))
+            band(w3, n * half + 64 * zi, wide, 32, 0, 32, coarse, plain_pick(q, zi))
             w3[n * half + 64 * zi + 32 : n * half + 64 * zi + 64, :] = jnp.zeros((32, full), BF)
     spread(wide, k4[...])
     for n, q in enumerate(order):
         for zi in range(levels // 2):
-            band(w4, n * half + 64 * zi, wide, 64, 0, 64, full, half, 64, plain_pick(q, zi))
+            band(w4, n * half + 64 * zi, wide, 64, 0, 64, coarse, plain_pick(q, zi))
     spread(wide, k5[...])
     for n, q in enumerate(order):
         for zi in range(levels):
-            band(w5, n * half + 32 * zi, wide, 96, 64, 32, full, half, 32, plain_pick(q, zi))
+            band(w5, n * half + 32 * zi, wide, 96, 64, 32, fine, plain_pick(q, zi))
     for n, d in enumerate((-1, 0, 1)):
         for zp in range(levels // 2):
             band(
-                w5, (4 + n) * half + 64 * zp, wide, 96, 0, 64, full, half, 32,
-                up_pick(d, zp, levels),
+                w5, (4 + n) * half + 64 * zp, wide, 96, 0, 64, fine,
+                up_pick(d, zp), False,
             )
 
     def pieces(count, rows):
@@ -318,11 +309,14 @@
 
         inner = pairs - 2 * margin
         blocks = inner // BLOCK
-        line, lane = iota((full, half), 0), iota((full, half), 1)
-        aim = (line % half) // 32 * 32 + line // half
+        line = iota((full, 1), 0)
+        ahead = iota((full, half), 1) - ((line % half) // 32 * 32 + line // half)
+        same = line % 32 == iota((1, 32), 1)
+        column = jnp.sum(jnp.where(same, tail[...].astype(F32), 0.0), axis=1, keepdims=True)
+        column = jnp.broadcast_to(column, (full, half))
 
         def add(m, head):
-            weight = jnp.where(lane == aim + 2 * m, tail[...].astype(F32), 0.0).astype(BF)
+            weight = jnp.where(ahead == 2 * m, column, 0.0).astype(BF)
             x = jnp.concatenate([d2[b * BLOCK + m, 0:rows] for b in range(blocks)], axis=0)
             return head + dot(x, weight)
 
@@ -330,26 +324,28 @@
         head = lax.fori_loop(0, BLOCK, add, zero, unroll=small)
         parts_per = BLOCK // per_chunk
         first = margin // per_chunk
-        line, lane = iota((128, half), 0), iota((128, half), 1)
+        line = iota((128, 1), 0)
         pair, q, z = line // window, (line % window) // levels, line % levels
+        aim = jnp.where((q > 0) & (q < 3), z * 32 + 2 * pair + q - 1, -4 * half)
+        past = iota((128, half), 1) - aim
         picture = jnp.zeros((blocks * rows, half), F32)
         for i in range(parts_per):
-            hit = (q > 0) & (q < 3) & (lane == z * 32 + 2 * (i * per_chunk + pair) + q - 1)
-            pickout = jnp.where(hit, 1.0, 0.0).astype(BF)
+            pickout = jnp.where(past == 2 * i * per_chunk, 1.0, 0.0).astype(BF)
             x = jnp.concatenate([u[first + b * parts_per + i] for b in range(blocks)], axis=0)
             picture = picture + dot(x, pickout)
         return head, picture, blocks
 
     def windows(source, deep, rows, pairs, offset):
         strip = min(pairs * window, 1024)
-        lane, col = iota((deep, strip), 0), iota((deep, strip), 1)
-        ahead = lane - offset - 2 * (col // window) - (col % window) // levels
+        lane, col = iota((deep, strip), 0), iota((1, strip), 1)
+        reach = offset + 2 * (col // window) + (col % window) // levels
+        level = col % levels
         chunks = []
         for start in range(0, pairs * window, strip):
 
             def add(z, total, start=start):
-                hit = (ahead == 2 * (start // window)) & (col % levels == z)
-                return total + dot(source(z), jnp.where(hit, 1.0, 0.0).astype(BF))
+                spot = jnp.where(level == z, reach + 2 * (start // window), -1)
+                return total + dot(source(z), jnp.where(lane == spot, 1.0, 0.0).astype(BF))
 
             zero = jnp.zeros((rows, strip), F32)
             total = lax.fori_loop(0, levels, add, zero, unroll=small)
@@ -390,39 +386,42 @@
             ref[1 + n - h : 1 + n, 0:yd] = zero
 
     head, picture, blocks = network(u, yd, pairs_x, HALO, clear)
-    flag = jnp.concatenate([xz_flag[...]] * blocks, axis=0)
-    done = jnp.where(flag[:, 0:1] > 0, picture + head, picture).astype(BF)
+    same = iota((yd, yd), 0) == iota((yd, yd), 1)
+    flag = jnp.sum(jnp.where(same, xz_flag[...].astype(F32), 0.0), axis=1, keepdims=True)
+    flag = jnp.concatenate([flag] * blocks, axis=0)
+    done = jnp.where(flag > 0, picture + head, picture).astype(BF)
     done = done.reshape(blocks, yd, half)
     span = xr.shape[-1]
     per = min(4, blocks)
     skew = lax.rem(g * width, 128)
-    line, lane = iota((half, levels * 128), 0), iota((half, levels * 128), 1)
+    line = iota((half, 1), 0)
+    past = iota((half, levels * 128), 1) - (line // 32 * 128 + skew + line % 32)
     for n in range(span // 128):
         total = jnp.zeros((yd, levels * 128), F32)
         for b in range(per):
-            hit = lane == line // 32 * 128 + skew + 32 * b + line % 32
-            total = total + dot(done[n * per + b], jnp.where(hit, 1.0, 0.0).astype(BF))
+            hit = jnp.where(past == 32 * b, 1.0, 0.0).astype(BF)
+            total = total + dot(done[n * per + b], hit)
         total = total.astype(BF)
         for z in range(levels):
             xr[z, :, 128 * n : 128 * (n + 1)] = total[:, 128 * z : 128 * (z + 1)]
 
     def xo(k):
         return pltpu.make_async_remote_copy(
-            src_ref=xr.at[pl.ds(k // chs * zd, zd)],
+            src_ref=xr.at[pl.ds(lax.div(k, chs) * zd, zd)],
             dst_ref=rx.at[g],
             send_sem=xo_send.at[k],
             recv_sem=xo_recv.at[g],
-            device_id={"slab": k // chs, "tile": t, "ch": k % chs},
+            device_id={"slab": lax.div(k, chs), "tile": t, "ch": lax.rem(k, chs)},
             device_id_type=MESH,
         )
 
     def xo_from(k):
         return pltpu.make_async_remote_copy(
-            src_ref=xr.at[pl.ds(k // chs * zd, zd)],
+            src_ref=xr.at[pl.ds(lax.div(k, chs) * zd, zd)],
             dst_ref=rx.at[k],
             send_sem=xo_send.at[k],
             recv_sem=xo_recv.at[k],
-            device_id={"slab": k // chs, "tile": t, "ch": k % chs},
+            device_id={"slab": lax.div(k, chs), "tile": t, "ch": lax.rem(k, chs)},
             device_id_type=MESH,
         )
 
@@ -446,7 +445,10 @@
     head, picture, blocks = network(u, rows_y, pairs_y, 0, lambda ref, by=1: None)
     row = iota((rows_y, 1), 0) + row_start
     mine = (row >= in_block) & (row < in_block + cols)
-    flag = yz_flag[pl.ds(row_start, rows_y), 0:1]
+    held = yz_flag.shape[1]
+    shift = row_start - lax.rem(place_me * held, 128)
+    same = iota((rows_y, held), 0) + shift == iota((rows_y, held), 1)
+    flag = jnp.sum(jnp.where(same, yz_flag[...].astype(F32), 0.0), axis=1, keepdims=True)
     for b in range(blocks):
         a = slice(b * rows_y, (b + 1) * rows_y)
         got = jnp.where(flag > 0, picture[a] + head[a], picture[a])
@@ -459,7 +461,7 @@
     def yo(k):
         ks, kt, kc = coords(k)
         return pltpu.make_async_remote_copy(
-            src_ref=yt.at[kt // fold, pl.ds(ks * zd, zd), lax.rem(kt, fold)],
+            src_ref=yt.at[lax.div(kt, fold), pl.ds(ks * zd, zd), lax.rem(kt, fold)],
             dst_ref=ry.at[me],
             send_sem=yo_send.at[k],
             recv_sem=yo_recv.at[me],
@@ -470,7 +472,7 @@
     def yo_from(k):
         ks, kt, kc = coords(k)
         return pltpu.make_async_remote_copy(
-            src_ref=yt.at[kt // fold, pl.ds(ks * zd, zd), lax.rem(kt, fold)],
+            src_ref=yt.at[lax.div(kt, fold), pl.ds(ks * zd, zd), lax.rem(kt, fold)],
             dst_ref=ry.at[k],
             send_sem=yo_send.at[k],
             recv_sem=yo_recv.at[k],
@@ -521,15 +523,9 @@
     rows = max(yd, rows_y)
     most = max(width // 2 + 2 * HALO, breadth // 2)
     span = max(128, width)
-    held = cols * chs
-    place = lax.axis_index("slab") * tiles + lax.axis_index("tile")
-    xz_flag = jnp.broadcast_to(xz_tissue[:, None], (yd, 128))
-    spot = lax.rem(place * held, 128)
-    yz_flag = lax.dynamic_update_slice(
-        jnp.zeros((128,), jnp.int32), yz_tissue, (spot,)
-    )
-    yz_flag = jnp.broadcast_to(yz_flag[:, None], (128, 128))
-    tail = jnp.broadcast_to(jnp.tile(out_weight, 2 * levels)[:, None], (full, half))
+    xz_flag = xz_tissue.reshape(1, -1)
+    yz_flag = yz_tissue.reshape(1, -1)
+    tail = out_weight.reshape(1, -1)
     first = jnp.pad(taps_first(first_conv), ((0, 7), (0, 0)))
     dma = pltpu.SemaphoreType.DMA
     vmem = pl.BlockSpec(memory_space=pltpu.VMEM)

time: 37.6 us -> 37 us (0.984)
  local copies, waits for them, and re-layouts: 8.28 us -> 6.87 us
  Pallas kernels: 28.7 us -> 29.8 us
    broadcast_in_dim x5 -> x0, local copies, waits for them, and re-layouts: 2.18 us -> none  [the longest x2 0.8 us: per_device(): jnp.broadcast_to(jnp.tile(out_weight, 2 * levels)[:, None], (full, half))]
    pallas_call x1, Pallas kernels: 28.7 us -> 29.8 us  [per_device(): pl.pallas_call(functools.partial(kernel, slabs, tiles, chs), out_shape=ja...]
    transpose x4, local copies, waits for them, and re-layouts: 3.08 us -> 4.02 us  [taps_first(): return jnp.transpose(weight, (1, 2, 0)).reshape(-1, weight.shape[0])]
    unnamed x17 -> x9, local copies, waits for them, and re-layouts: 2.24 us -> 2.25 us
where the time goes in v2:
time: 37 us; the launch traced here: 36.7 us
  Pallas kernels  29.8 us (81%)
  local copies, waits for them, and re-layouts  6.87 us (19%)
    pallas_call x1, Pallas kernels, per_device(): pl.pallas_call(functools.partial(kernel, slabs, tiles, chs), out_shape=ja...  29.8 us
    transpose x4, local copies, waits for them, and re-layouts, taps_first(): return jnp.transpose(weight, (1, 2, 0)).reshape(-1, weight.shape[0])  4.02 us
    unnamed x9, local copies, waits for them, and re-layouts  2.25 us

profile of v2, /device:TPU:0, one launch (start us, length us, event | category | flops | bytes accessed | tf_op | source)
XLA Modules:
  0.0 36.7 jit_solution(18149649293525344502)
XLA Ops:
  0.0 0.0 copy-start.3
  0.0 0.7 %copy-done.3 = bf16[32,9,1]{0,1,2:T(8,128)(2,1)S(1)} copy-done((bf16[32,9,1]{0,1,2:T(8,128)(2,1)S(1)}, bf16[32,9,1]{0,1,2:T(8,128)(2,1)}, u32[]{:S(2)}) %copy-start.3) | copy-done | bytes 600
  0.7 0.0 copy-start.1
  0.7 0.6 %pad.4.k1 = bf16[16,32]{1,0:T(8,128)(2,1)} pad(bf16[9,32]{1,0:T(8,128)(2,1)S(1)} %bitcast.26, bf16[]{:T(256)} %constant.2.clone.1), padding=0_7x0_0 | pad | bytes 1602 | tf_op jit(solution)/shard_map/jit(_pad)/pad | solution.py:529
  1.3 0.0 copy-start
  1.3 1.6 %copy.11 = bf16[9,32,32]{2,1,0:T(8,128)(2,1)} copy(bf16[9,32,32]{1,2,0:T(8,128)(2,1)} %bitcast.23) | data formatting | bytes 36864 | tf_op jit(solution)/shard_map/transpose | solution.py:509
  2.9 0.0 copy-done.1
  2.9 0.7 %copy.14 = bf16[9,32,32]{2,1,0:T(8,128)(2,1)} copy(bf16[9,32,32]{1,2,0:T(8,128)(2,1)S(1)} %bitcast.24) | data formatting | bytes 36864 | tf_op jit(solution)/shard_map/transpose | solution.py:509
  3.7 0.0 copy-done
  3.7 0.0 copy-start.2
  3.7 0.8 %copy.12 = bf16[9,64,64]{2,1,0:T(8,128)(2,1)} copy(bf16[9,64,64]{1,2,0:T(8,128)(2,1)S(1)} %bitcast.21) | data formatting | bytes 147456 | tf_op jit(solution)/shard_map/transpose | solution.py:509
  4.5 0.1 copy-done.2
  4.6 0.8 %copy.13 = bf16[9,96,32]{2,1,0:T(8,128)(2,1)} copy(bf16[9,96,32]{1,2,0:T(8,128)(2,1)S(1)} %bitcast.25) | data formatting | bytes 110592 | tf_op jit(solution)/shard_map/transpose | solution.py:509
  5.4 29.8 %shard_map.100 = bf16[2,16,1024]{2,1,0:T(8,128)(2,1)} custom-call(bf16[2,16,1024]{2,1,0:T(8,128)(2,1)} %vol.1, s32[1,16]{1,0:T(1,128)} %bitcast.27, s32[1,64]{1,0:T(1,128)} %bitcast.28, bf16[16,32]{1,0:T(8,128)(2,1)} %pad.4.k1, bf16[288,32]{1,0:T(8,128)(2,1)} %bitcast.19, bf16[288,64]{1,0:T(8,128)(2,1)} %bitcast.22, bf16[576,64]{1,0:T(8,128)(2,1)} %bitcast.18, ...), custom_call_target="tpu_custom_call" | custom-call | tf_op jit(solution)/shard_map/pallas_call | solution.py:536
  35.2 1.5 %copy.16 = bf16[2,16,1024]{2,1,0:T(8,128)(2,1)} copy(bf16[2,16,1024]{2,1,0:T(8,128)(2,1)} %shard_map.100) | data formatting | bytes 131072
Async XLA Ops:
  0.0 0.7 %copy-start.3 = (bf16[32,9,1]{0,1,2:T(8,128)(2,1)S(1)}, bf16[32,9,1]{0,1,2:T(8,128)(2,1)}, u32[]{:S(2)}) copy-start(bf16[32,9,1]{0,1,2:T(8,128)(2,1)} %param.13) | copy-start | bytes 1732
  0.7 2.3 %copy-start.1 = (bf16[32,9,32]{2,0,1:T(8,128)(2,1)S(1)}, bf16[32,9,32]{2,0,1:T(8,128)(2,1)}, u32[]{:S(2)}) copy-start(bf16[32,9,32]{2,0,1:T(8,128)(2,1)} %param.18) | copy-start | bytes 55300
  1.3 2.4 %copy-start = (bf16[64,9,64]{2,0,1:T(8,128)(2,1)S(1)}, bf16[64,9,64]{2,0,1:T(8,128)(2,1)}, u32[]{:S(2)}) copy-start(bf16[64,9,64]{2,0,1:T(8,128)(2,1)} %param.16) | copy-start | bytes 221188
  3.7 0.9 %copy-start.2 = (bf16[32,9,96]{2,0,1:T(8,128)(2,1)S(1)}, bf16[32,9,96]{2,0,1:T(8,128)(2,1)}, u32[]{:S(2)}) copy-start(bf16[32,9,96]{2,0,1:T(8,128)(2,1)} %param.17) | copy-start | bytes 165892
